TPU v7x, 256 devices: a whole 4x4x8 slice. The times are simulated.
256 devices in a mesh: ty: 16 (over z_hi, y, core), tx: 16 (over x, z_lo).
Axes of the slice: x: 4, y: 4, z: 8 (z_hi: 2, z_lo: 4; z = z_hi * 4 + z_lo), core: 2. Of those that a mesh axis runs over, the one named last changes fastest.
Arguments:
- object_field: float32 [2, 8192, 8192], P(None, 'ty', 'tx'), may hold values from -5 to 5
- probe: float32 [2, 256, 256], replicated, may hold values from -5 to 5
- intensity: float32 [16, 16, 8, 256, 256], P('ty', 'tx'), may hold values from 0.05 to 4
- positions: int32 [2, 16, 16, 8], P(None, 'ty', 'tx'), may hold values from -128 to 384
- counts: int32 [16, 16], P('ty', 'tx'), may hold values from 1 to 8, as said below
Outputs:
- object_new: float32 [2, 8192, 8192], P(None, 'ty', 'tx')
- probe_new: float32 [2, 256, 256], replicated
Inputs may be any that keep to these rules, and one draw needn't show every extreme that they name: counts are skewed over tiles; some tile has 8.
All inputs are finite; a program needn't handle non-finite values.
Results may differ from a plain program's by a relative error of at most 0.00013.
Values sent between devices are 32-bit elements; how exact they have to be, the bound alone decides.
No kernel may reach another device: no remote copies, remote signals or barrier semaphores. Data moves between devices by JAX's collectives and lax.ppermute only.
A program may use at most 128 MiB of HBM per device.

v0:
```python
import numpy as np
import ml_dtypes
import jax
import jax.numpy as jnp
from jax import lax
from jax.experimental import pallas as pl
from jax.experimental.pallas import tpu as pltpu
from jax.sharding import PartitionSpec as P

BF16 = jnp.bfloat16
F32 = jnp.float32
LANES = 128
VMEM = pl.BlockSpec(memory_space=pltpu.VMEM)
SMEM = pl.BlockSpec(memory_space=pltpu.SMEM)
HBM = pl.BlockSpec(memory_space=pltpu.HBM)
def split_host(table):
    high = table.astype(ml_dtypes.bfloat16)
    low = (table - high.astype(np.float64)).astype(ml_dtypes.bfloat16)
    return high, low


def half_tables(size):
    half = size // 2
    left, right = [], []
    for parity in range(2):
        product = (2 * np.arange(half)[:, None] + parity) * np.arange(half)[None, :] % size
        angle = 2.0 * np.pi * product / size
        cos, sin = np.cos(angle) / np.sqrt(size), np.sin(angle) / np.sqrt(size)
        base = np.block([[cos, sin], [-sin, cos]])
        for table in (base, base.T):
            high, low = split_host(table)
            left.append(np.concatenate([high, high, low], axis=1))
            right.append(np.concatenate([high, high, low], axis=0))
    return np.stack(left), np.stack(right)


def parity_tables(size):
    order = np.concatenate([np.arange(0, size, 2), np.arange(1, size, 2)])
    gather = np.eye(size)[order].astype(ml_dtypes.bfloat16)
    return np.concatenate([gather] * 3, axis=1), np.concatenate([gather.T] * 3, axis=0)


def matmul(left, right):
    return jnp.dot(left, right, preferred_element_type=F32)


def split(value):
    high = value.astype(BF16)
    return high, (value - high.astype(F32)).astype(BF16)


def put_rows(ref, start, columns, value):
    rows = value.shape[0]
    high, low = split(value)
    third = ref.shape[0] // 3
    ref[start : start + rows, columns] = high
    ref[third + start : third + start + rows, columns] = low
    ref[2 * third + start : 2 * third + start + rows, columns] = high


def put_columns(ref, rows, start, value):
    width = value.shape[1]
    high, low = split(value)
    third = ref.shape[1] // 3
    ref[rows, start : start + width] = high
    ref[rows, third + start : third + start + width] = low
    ref[rows, 2 * third + start : 2 * third + start + width] = high


def place(row, col, last):
    tile = jnp.minimum(lax.shift_right_logical(col, 7), last)
    return row, tile, col - tile * LANES


def add_window(accumulate, row, tile, offset, first, second):
    rows = first.shape[0]
    turn = jnp.bitwise_and(offset, LANES - 1)
    kept = lax.broadcasted_iota(jnp.int32, first.shape, 1) >= offset
    first = pltpu.roll(first, turn, 1)
    second = pltpu.roll(second, turn, 1)
    where = pl.ds(row, rows)
    accumulate[tile, where, :] += jnp.where(kept, first, 0.0)
    accumulate[tile + 1, where, :] += jnp.where(kept, second, first)
    accumulate[tile + 2, where, :] += jnp.where(kept, 0.0, second)


def fold_kernel(count, measured, gather_left, gather_right, folded, parts):
    size = measured.shape[1]

    def three(value):
        high = value.astype(BF16)
        rest = value - high.astype(F32)
        middle = rest.astype(BF16)
        return high, middle, (rest - middle.astype(F32)).astype(BF16)

    def step(slot, carry):
        for index, part in enumerate(three(measured[slot])):
            parts[:, index * size : (index + 1) * size] = part
        value = matmul(parts[...], gather_right[...])
        folded[slot] = matmul(gather_left[...], jnp.concatenate(three(value), axis=0))
        return carry

    lax.fori_loop(0, count[0], step, 0)


def own_notes(position, count):
    row = lax.broadcasted_iota(jnp.int32, (8, LANES), 0)
    lane = lax.broadcasted_iota(jnp.int32, (8, LANES), 1)
    notes = jnp.where(row == 2, count[0], 0)
    for slot in range(position.shape[1]):
        for axis in range(2):
            notes = jnp.where((row == axis) & (lane == slot), position[axis, slot], notes)
    return notes.astype(F32)


def edge_kernel(odd, position, count, tile_ref, x_first, x_second, y_first, y_second):
    half = LANES
    side = tile_ref.shape[1]
    odd_y, odd_x = odd[0] == 1, odd[1] == 1
    notes = own_notes(position, count)
    low, high = tile_ref[:, :, :half], tile_ref[:, :, side - half :]
    x_first[:, :side, :] = jnp.where(odd_x, high, low)
    x_second[:, :side, :] = jnp.where(odd_x, low, high)
    for out in (x_first, x_second):
        for plane in range(2):
            out[plane, side:, :] = notes
    low, high = tile_ref[:, :half, :], tile_ref[:, side - half :, :]
    y_first[...] = jnp.where(odd_y, high, low)
    y_second[...] = jnp.where(odd_y, low, high)


def corner_kernel(odd, position, count, x_first, x_second, after, first, second):
    half = LANES
    side = x_first.shape[1] - 8
    far = side - half
    odd_x = odd[1] == 1
    notes = own_notes(position, count)
    for out, odd_start in ((first, far), (second, 0)):
        rows = pl.ds(pl.multiple_of(jnp.where(odd[0] == 1, odd_start, far - odd_start), LANES), half)
        for index, (even_ref, odd_ref) in enumerate(((x_first, x_second), (x_second, x_first))):
            out[:, index, :half, :] = jnp.where(odd_x, odd_ref[:, rows, :], even_ref[:, rows, :])
            out[:, index, half : half + 8, :] = jnp.where(odd_x, odd_ref[:, side:, :], even_ref[:, side:, :])
            for plane in range(2):
                out[plane, index, half + 8 :, :] = notes


def slot_stages(row, tile, offset, live, probe, measured, left, right, canvas, grad, probe_sum, patch, rhs, lhs):
    size = probe.shape[1]
    half = size // 2
    near, far = slice(0, half), slice(half, size)
    turn = jnp.bitwise_and(LANES - offset, LANES - 1)
    kept = lax.broadcasted_iota(jnp.int32, (size, LANES), 1) < LANES - offset
    for plane in range(2):
        raw = [pltpu.roll(canvas[plane, tile + index, pl.ds(row, size), :], turn, 1) for index in range(3)]
        patch[plane, 0] = jnp.where(kept, raw[0], raw[1])
        patch[plane, 1] = jnp.where(kept, raw[1], raw[2])
    for index, columns in enumerate((near, far)):
        probe_re, probe_im = probe[0, :, columns], probe[1, :, columns]
        patch_re, patch_im = patch[0, index], patch[1, index]
        exit_re = probe_re * patch_re - probe_im * patch_im
        exit_im = probe_re * patch_im + probe_im * patch_re
        probe_sum[2, index] += (patch_re * patch_re + patch_im * patch_im) * live
        put_rows(rhs.at[0], 0, columns, exit_re[:half] + exit_re[half:])
        put_rows(rhs.at[0], half, columns, exit_im[:half] + exit_im[half:])
        put_rows(rhs.at[1], 0, columns, exit_re[:half] - exit_re[half:])
        put_rows(rhs.at[1], half, columns, exit_im[:half] - exit_im[half:])
    yield
    for parity in range(2):
        value = matmul(left[2 * parity], rhs[parity])
        rows = slice(parity * half, (parity + 1) * half)
        put_columns(lhs.at[0], rows, 0, value[:half, near] + value[:half, far])
        put_columns(lhs.at[0], rows, half, value[half:, near] + value[half:, far])
        put_columns(lhs.at[1], rows, 0, value[:half, near] - value[:half, far])
        put_columns(lhs.at[1], rows, half, value[half:, near] - value[half:, far])
        yield
    everything = slice(0, size)
    for parity in range(2):
        value = matmul(lhs[parity], right[2 * parity + 1])
        wave_re, wave_im = value[:, near], value[:, far]
        columns = slice(parity * half, (parity + 1) * half)
        excess = (wave_re * wave_re + wave_im * wave_im - measured[:, columns]) * live
        put_columns(lhs.at[parity], everything, 0, excess * wave_re)
        put_columns(lhs.at[parity], everything, half, excess * wave_im)
        yield
    back = []
    for parity in range(2):
        back.append(matmul(lhs[parity], right[2 * parity]))
    for parity in range(2):
        rows = slice(parity * half, (parity + 1) * half)
        put_rows(rhs.at[parity], 0, near, back[0][rows, near] + back[1][rows, near])
        put_rows(rhs.at[parity], half, near, back[0][rows, far] + back[1][rows, far])
        put_rows(rhs.at[parity], 0, far, back[0][rows, near] - back[1][rows, near])
        put_rows(rhs.at[parity], half, far, back[0][rows, far] - back[1][rows, far])
    yield
    even = matmul(left[1], rhs[0])
    odd = matmul(left[3], rhs[1])
    pieces = []
    for index, columns in enumerate((near, far)):
        chi_re, chi_im = (
            jnp.concatenate([even[rows, columns] + odd[rows, columns], even[rows, columns] - odd[rows, columns]], axis=0)
            for rows in (near, far)
        )
        probe_re, probe_im = probe[0, :, columns], probe[1, :, columns]
        patch_re, patch_im = patch[0, index], patch[1, index]
        probe_sum[0, index] += patch_re * chi_re + patch_im * chi_im
        probe_sum[1, index] += patch_re * chi_im - patch_im * chi_re
        pieces.append((probe_re * chi_re + probe_im * chi_im, probe_re * chi_im - probe_im * chi_re))
    for plane in range(2):
        add_window(grad.at[plane], row, tile, offset, pieces[0][plane], pieces[1][plane])
    yield


def run_slots(wanted, position, count, probe, folded, left, right, canvas, grad, probe_sum, order, patch, rhs, lhs):
    size = probe.shape[1]
    half = size // 2
    tiles = canvas.shape[1] - 2
    reach = tiles * LANES - size

    def pick(slot, found):
        row, col = position[0, slot], position[1, slot]
        take = wanted((row >= 0) & (row <= reach), (col >= 0) & (col <= reach))

        @pl.when(take)
        def keep():
            order[found] = slot

        return found + jnp.where(take, 1, 0)

    total = lax.fori_loop(0, count[0], pick, 0)
    lanes = patch.shape[0]

    def step(group, carry):
        stages = []
        for lane in range(lanes):
            index = lanes * group + lane
            live = jnp.where(index < total, 1.0, 0.0)
            slot = order[jnp.minimum(index, total - 1)]
            row, tile, offset = place(position[0, slot] + half, position[1, slot] + half, tiles - 1)
            stages.append(slot_stages(
                row, tile, offset, live, probe, folded.at[slot], left, right, canvas, grad, probe_sum,
                patch.at[lane], rhs.at[lane], lhs.at[lane],
            ))
        for _ in zip(*stages):
            pass
        return carry

    lax.fori_loop(0, lax.div(total + (lanes - 1), lanes), step, 0)


def core_kernel(odd, position, count, probe, folded, left, right, tile_ref, canvas, grad, probe_sum, token, *scratch):
    side = tile_ref.shape[1]
    half = LANES
    tiles = side // LANES
    canvas[...] = jnp.zeros_like(canvas)
    for index in range(tiles):
        canvas[:, 1 + index, half : half + side, :] = tile_ref[:, :, index * LANES : (index + 1) * LANES]
    grad[...] = jnp.zeros_like(grad)
    probe_sum[...] = jnp.zeros_like(probe_sum)
    token[...] = jnp.zeros_like(token)
    run_slots(lambda row, col: row & col, position, count, probe, folded, left, right, canvas, grad, probe_sum, *scratch)


def column_slots_kernel(
    odd, position, count, probe, folded, left, right, x_first, x_second, canvas_in, grad_in, sum_in,
    canvas, grad, probe_sum, *scratch,
):
    side = x_first.shape[1] - 8
    half = LANES
    last = canvas.shape[1] - 1
    inner = slice(half, half + side)
    odd_x = odd[1] == 1
    canvas[:, 0, inner, :] = jnp.where(odd_x, x_second[:, :side, :], x_first[:, :side, :])
    canvas[:, last, inner, :] = jnp.where(odd_x, x_first[:, :side, :], x_second[:, :side, :])
    run_slots(
        lambda row, col: row & jnp.logical_not(col),
        position, count, probe, folded, left, right, canvas, grad, probe_sum, *scratch,
    )


def row_kernel(
    odd, position, count, probe, folded, left, right, y_first, y_second, canvas_in, grad_in, sum_in,
    canvas, grad, probe_sum, *scratch,
):
    half = LANES
    side = y_first.shape[2]
    odd_y = odd[0] == 1
    for index in range(side // LANES):
        columns = slice(index * LANES, (index + 1) * LANES)
        canvas[:, 1 + index, :half, :] = jnp.where(odd_y, y_second[:, :, columns], y_first[:, :, columns])
        canvas[:, 1 + index, half + side :, :] = jnp.where(odd_y, y_first[:, :, columns], y_second[:, :, columns])
    run_slots(
        lambda row, col: jnp.logical_not(row) & col,
        position, count, probe, folded, left, right, canvas, grad, probe_sum, *scratch,
    )


def outer_kernel(
    odd, position, count, probe, folded, left, right, x_first, x_second, corner_first, corner_second,
    canvas_in, grad_in, sum_in,
    margin_first, margin_second, side_low, side_high, middle, sums, places, canvas, grad, probe_sum, sems, *scratch,
):
    size = probe.shape[1]
    half = size // 2
    side = x_first.shape[1] - 8
    tiles = side // LANES
    inner = slice(half, half + side)
    odd_y, odd_x = odd[0] == 1, odd[1] == 1
    for index, tile in enumerate((0, 1 + tiles)):
        above, below = corner_first[:, index, :half, :], corner_second[:, index, :half, :]
        canvas[:, tile, :half, :] = jnp.where(odd_y, below, above)
        canvas[:, tile, half + side :, :] = jnp.where(odd_y, above, below)
    run_slots(
        lambda row, col: jnp.logical_not(row | col),
        position, count, probe, folded, left, right, canvas, grad, probe_sum, *scratch,
    )
    copies = []

    def send(source, target):
        copy = pltpu.make_async_copy(source, target, sems.at[len(copies)])
        copy.start()
        copies.append(copy)

    for out, odd_start in ((margin_first, half + side), (margin_second, 0)):
        rows = pl.ds(pl.multiple_of(jnp.where(odd_y, odd_start, half + side - odd_start), LANES), half)
        send(grad.at[:, :, rows, :], out)
    send(grad.at[:, 0, inner, :], side_low)
    send(grad.at[:, 1 + tiles, inner, :], side_high)
    send(grad.at[:, 1 : 1 + tiles, inner, :], middle)
    for plane in range(3):
        for index in range(2):
            sums[:, 2 * plane + index] = probe_sum[plane, index].reshape(size // 8, 8, LANES)
    beside, own = slice(half, half + 8), slice(half + 8, half + 16)
    for start, (even_ref, odd_ref) in ((0, (corner_first, corner_second)), (6, (corner_second, corner_first))):
        for index, (tile, rows) in enumerate(((0, beside), (0, own), (1, beside))):
            places[start + index] = jnp.where(odd_y, odd_ref[0, tile, rows, :], even_ref[0, tile, rows, :])
    places[3] = jnp.where(odd_x, x_second[0, side:, :], x_first[0, side:, :])
    places[4] = own_notes(position, count)
    places[5] = jnp.where(odd_x, x_first[0, side:, :], x_second[0, side:, :])
    for copy in copies:
        copy.wait()


def sides_kernel(odd, own_low, own_high, low_first, low_second, high_first, high_second, after, first, second, token):
    half = LANES
    side = own_low.shape[1]
    odd_y, odd_x = odd[0] == 1, odd[1] == 1
    for start in range(0, side, half):
        rows = slice(start, start + half)
        values = []
        for own, y_first, y_second in ((own_low, low_first, low_second), (own_high, high_first, high_second)):
            value = own[:, rows, :]
            if start == 0:
                value = value + jnp.where(odd_y, y_second[:, 0], y_first[:, 0])
            if start + half == side:
                value = value + jnp.where(odd_y, y_first[:, 0], y_second[:, 0])
            values.append(value)
        first[:, rows, :] = jnp.where(odd_x, values[1], values[0])
        second[:, rows, :] = jnp.where(odd_x, values[0], values[1])
    token[...] = jnp.zeros_like(token)


def weight_kernel(numbers, probe, scale, power, weight):
    half = LANES
    side = scale.shape[1]
    tiles = side // LANES
    weight[...] = jnp.zeros_like(weight)
    for index in range(2):
        columns = slice(index * LANES, (index + 1) * LANES)
        power[index] = probe[0, :, columns] * probe[0, :, columns] + probe[1, :, columns] * probe[1, :, columns]
    for index in range(9):
        down, across = index // 3 - 1, index % 3 - 1

        def step(slot, carry):
            row = numbers[index, 0, slot].astype(jnp.int32) + (2 * half + down * side)
            col = numbers[index, 1, slot].astype(jnp.int32) + (2 * half + across * side)
            reach = side + 2 * half

            @pl.when((row > 0) & (row < reach) & (col > 0) & (col < reach))
            def add():
                at, tile, offset = place(row, col, tiles + 1)
                add_window(weight, at, tile, offset, power[0], power[1])

            return carry

        lax.fori_loop(0, numbers[index, 2, 0].astype(jnp.int32), step, 0)
    for index in range(tiles):
        scale[index] = 1.0 / (weight[2 + index, 2 * half : 2 * half + side, :] + 1.0)


def update_kernel(odd, tile_ref, grad, y_first, y_second, scale, out):
    half = LANES
    side = tile_ref.shape[1]
    odd_y = odd[0] == 1
    for plane in range(2):
        for start in range(0, side, half):
            rows = slice(start, start + half)
            value = grad[plane, 0, rows, :]
            if start == 0:
                value = value + jnp.where(odd_y, y_second[plane, 0], y_first[plane, 0])
            if start + half == side:
                value = value + jnp.where(odd_y, y_first[plane, 0], y_second[plane, 0])
            out[plane, rows, :] = tile_ref[plane, rows, :] - value * scale[0, rows, :]


def column_kernel(odd, before, x_first, x_second, scale, out):
    use_first = odd[1] == pl.program_id(0)
    for plane in range(2):
        out[plane] = before[plane] - jnp.where(use_first, x_first[plane], x_second[plane]) * scale[0]


def plane_kernel(parts, after, later, out):
    out[...] = jnp.broadcast_to(jnp.sum(parts[...], axis=0)[None], out.shape)


def probe_kernel(index, parts, probe, after, out):
    total = jnp.sum(parts[...], axis=0)
    rows = pl.ds(pl.multiple_of(index[0] * 8, 8), 8)
    for tile in range(2):
        root = jnp.sqrt(total[4 + tile] + 1.0)
        for plane in range(2):
            new = probe[plane, rows, tile * LANES : (tile + 1) * LANES] - total[2 * plane + tile] / root
            out[:, 2 * plane + tile] = jnp.broadcast_to(new[None], (out.shape[0], 8, LANES))


def join_kernel(pieces, out):
    for plane in range(2):
        for tile in range(2):
            value = pieces[:, 2 * plane + tile]
            out[plane, :, tile * LANES : (tile + 1) * LANES] = value.reshape(out.shape[1], LANES)


def swap(first, second, axis):
    count = lax.axis_size(axis)
    across = [pair for low in range(1, count - 1, 2) for pair in ((low, low + 1), (low + 1, low))]
    return lax.ppermute(first, axis, across), lax.ppermute(second, axis, [(index, index ^ 1) for index in range(count)])


def keep(value):
    return pltpu.with_memory_space_constraint(value, pltpu.HBM)


def params(mib):
    return pltpu.CompilerParams(vmem_limit_bytes=mib * 2**20)


def cost(mib):
    return pl.CostEstimate(flops=0, bytes_accessed=mib * 2**20, transcendentals=0)


def solution(mesh):
    rows, cols = mesh.shape["ty"], mesh.shape["tx"]
    near_y, near_z = 8, 4
    planes = [
        [(8 * high + row) * cols + near_z * x + low for row in range(near_y) for x in range(cols // near_z)]
        for high in range(rows // near_y)
        for low in range(near_z)
    ]
    lines = [list(line) for line in zip(*planes)]

    def trade(pieces, groups):
        return lax.all_to_all(pieces, ("ty", "tx"), 0, 0, axis_index_groups=groups, tiled=True)

    def per_device(object_field, probe, intensity, positions, counts):
        side = object_field.shape[1]
        size = probe.shape[1]
        half = size // 2
        slots = intensity.shape[2]
        tiles = side // LANES
        position = positions[:, 0, 0, :]
        count = counts[0]
        row, col = lax.axis_index("ty"), lax.axis_index("tx")
        piece = jnp.bitwise_and(row, near_y - 1) * (cols // near_z) + lax.shift_right_logical(col, 2)
        piece = piece.reshape(1).astype(jnp.int32)
        left, right = (jnp.asarray(table) for table in half_tables(size))
        gather_left, gather_right = (jnp.asarray(table) for table in parity_tables(size))

        odd = jnp.bitwise_and(jnp.stack([row, col]), 1).astype(jnp.int32)

        strip = jax.ShapeDtypeStruct((2, side + 8, LANES), F32)
        edge = jax.ShapeDtypeStruct((2, half, side), F32)
        x_first, x_second, y_first, y_second = pl.pallas_call(
            edge_kernel,
            out_shape=(strip, strip, edge, edge),
            in_specs=[SMEM] * 3 + [VMEM],
            out_specs=(VMEM,) * 4,
            compiler_params=params(6),
            cost_estimate=cost(4),
            name="edges",
        )(odd, position, count, object_field)
        x_first, x_second = swap(x_first, x_second, "tx")
        y_first, y_second = swap(y_first, y_second, "ty")
        folded = pl.pallas_call(
            fold_kernel,
            out_shape=jax.ShapeDtypeStruct((slots, size, size), F32),
            in_specs=[SMEM, VMEM, VMEM, VMEM],
            out_specs=VMEM,
            scratch_shapes=[pltpu.VMEM((size, 3 * size), BF16)],
            compiler_params=params(8),
            cost_estimate=cost(6),
            name="fold",
        )(count, intensity[0, 0], gather_left, gather_right)
        members = len(planes[0])
        lanes = 2
        scratch = [
            pltpu.SMEM((slots,), jnp.int32),
            pltpu.VMEM((lanes, 2, 2, size, LANES), F32),
            pltpu.VMEM((lanes, 2, 3 * size, size), BF16),
            pltpu.VMEM((lanes, 2, size, 3 * size), BF16),
        ]
        state = (
            pltpu.VMEM((2, tiles + 2, side + size, LANES), F32),
            pltpu.VMEM((2, tiles + 2, side + size, LANES), F32),
            pltpu.VMEM((3, 2, size, LANES), F32),
        )
        given = (odd, position, count, probe, folded, left, right)
        canvas, grad, probe_sum, token = pl.pallas_call(
            core_kernel,
            out_shape=state + (jax.ShapeDtypeStruct((8, LANES), F32),),
            in_specs=[SMEM] * 3 + [VMEM] * 5,
            out_specs=(VMEM,) * 4,
            scratch_shapes=scratch,
            compiler_params=params(26),
            cost_estimate=cost(16),
            name="core_slots",
        )(*given, object_field)
        corner = jax.ShapeDtypeStruct((2, 2, half + 16, LANES), F32)
        corners = pl.pallas_call(
            corner_kernel,
            out_shape=(corner, corner),
            in_specs=[SMEM] * 3 + [VMEM] * 2 + [HBM],
            out_specs=(VMEM, VMEM),
            compiler_params=params(4),
            cost_estimate=cost(4),
            name="corners",
        )(odd, position, count, x_first, x_second, token)
        corners = swap(*corners, "ty")

        canvas, grad, probe_sum = pl.pallas_call(
            column_slots_kernel,
            out_shape=state,
            in_specs=[SMEM] * 3 + [VMEM] * 9,
            out_specs=(VMEM,) * 3,
            scratch_shapes=scratch,
            input_output_aliases={9: 0, 10: 1, 11: 2},
            compiler_params=params(26),
            cost_estimate=cost(16),
            name="column_slots",
        )(*given, x_first, x_second, canvas, grad, probe_sum)
        canvas, grad, probe_sum = pl.pallas_call(
            row_kernel,
            out_shape=state,
            in_specs=[SMEM] * 3 + [VMEM] * 9,
            out_specs=(VMEM,) * 3,
            scratch_shapes=scratch,
            input_output_aliases={9: 0, 10: 1, 11: 2},
            compiler_params=params(26),
            cost_estimate=cost(8),
            name="row_slots",
        )(*given, y_first, y_second, canvas, grad, probe_sum)
        margin = pltpu.HBM((2, tiles + 2, half, LANES), F32)
        column = pltpu.HBM((2, side, LANES), F32)
        margin_first, margin_second, side_low, side_high, middle, sums, places, *_ = pl.pallas_call(
            outer_kernel,
            out_shape=(
                margin, margin, column, column,
                pltpu.HBM((2, tiles, side, LANES), F32),
                pltpu.HBM((members, 6, 8, LANES), F32),
                jax.ShapeDtypeStruct((9, 8, LANES), F32),
            ) + state,
            in_specs=[SMEM] * 3 + [VMEM] * 11,
            out_specs=(HBM,) * 5 + (VMEM,) * 5,
            scratch_shapes=[pltpu.SemaphoreType.DMA((5,))] + scratch,
            input_output_aliases={11: 7, 12: 8, 13: 9},
            compiler_params=params(26),
            cost_estimate=cost(16),
            name="outer_slots",
        )(*given, x_first, x_second, *corners, canvas, grad, probe_sum)

        margin_first, margin_second = swap(margin_first, margin_second, "ty")
        scale = pl.pallas_call(
            weight_kernel,
            out_shape=jax.ShapeDtypeStruct((tiles, side, LANES), F32),
            in_specs=[SMEM, VMEM],
            out_specs=VMEM,
            scratch_shapes=[
                pltpu.VMEM((2, size, LANES), F32),
                pltpu.VMEM((tiles + 4, side + 2 * size, LANES), F32),
            ],
            compiler_params=params(8),
            cost_estimate=cost(8),
            name="weights",
        )(places, keep(probe))
        parts = trade(sums, planes)
        parts = pl.pallas_call(
            plane_kernel,
            out_shape=pltpu.HBM((len(lines[0]), 6, 8, LANES), F32),
            in_specs=[VMEM, HBM, HBM],
            out_specs=VMEM,
            compiler_params=params(6),
            cost_estimate=cost(2),
            name="plane_sum",
        )(parts, scale, margin_first)
        parts = trade(parts, lines)
        strip = pltpu.HBM((2, side, LANES), F32)
        whole = pl.BlockSpec((2, side, LANES), lambda index: (0, 0, 0))
        first_tile = pl.BlockSpec((2, 1, half, LANES), lambda index: (0, 0, 0, 0))
        last_tile = pl.BlockSpec((2, 1, half, LANES), lambda index: (0, tiles + 1, 0, 0))
        *margins, token = pl.pallas_call(
            sides_kernel,
            out_shape=(strip, strip, jax.ShapeDtypeStruct((8, LANES), F32)),
            grid=(1,),
            in_specs=[SMEM, whole, whole, first_tile, first_tile, last_tile, last_tile, HBM],
            out_specs=(whole, whole, pl.BlockSpec((8, LANES), lambda index: (0, 0))),
            compiler_params=params(8),
            cost_estimate=cost(16),
            name="sides",
        )(odd, keep(side_low), keep(side_high), margin_first, margin_second, margin_first, margin_second, parts)
        x_first, x_second = swap(*margins, "tx")

        pieces = pl.pallas_call(
            probe_kernel,
            out_shape=pltpu.HBM((members, 4, 8, LANES), F32),
            in_specs=[SMEM, VMEM, VMEM, HBM],
            out_specs=VMEM,
            compiler_params=params(6),
            cost_estimate=cost(2),
            name="probe_rows",
        )(piece, parts, keep(probe), token)
        probe_new = pl.pallas_call(
            join_kernel,
            out_shape=jax.ShapeDtypeStruct(probe.shape, F32),
            in_specs=[VMEM],
            out_specs=VMEM,
            compiler_params=params(6),
            cost_estimate=cost(2),
            name="join",
        )(trade(pieces, planes))

        column = pl.BlockSpec((2, side, LANES), lambda index: (0, 0, index))
        flat = pl.BlockSpec((2, 1, half, LANES), lambda index: (0, index + 1, 0, 0))
        object_new = pl.pallas_call(
            update_kernel,
            out_shape=jax.ShapeDtypeStruct(object_field.shape, F32),
            grid=(tiles,),
            in_specs=[
                SMEM, column, pl.BlockSpec((2, 1, side, LANES), lambda index: (0, index, 0, 0)), flat, flat,
                pl.BlockSpec((1, side, LANES), lambda index: (index, 0, 0)),
            ],
            out_specs=column,
            compiler_params=params(8),
            cost_estimate=cost(8),
            name="update",
        )(odd, keep(object_field), keep(middle), margin_first, margin_second, scale)
        ends = pl.BlockSpec((2, side, LANES), lambda index: (0, 0, index * (tiles - 1)))
        object_new = pl.pallas_call(
            column_kernel,
            out_shape=jax.ShapeDtypeStruct(object_field.shape, F32),
            grid=(2,),
            in_specs=[SMEM, ends, whole, whole, pl.BlockSpec((1, side, LANES), lambda index: (index * (tiles - 1), 0, 0))],
            out_specs=ends,
            input_output_aliases={1: 0},
            compiler_params=params(8),
            name="columns",
        )(odd, object_new, x_first, x_second, scale)
        return (object_new, probe_new)

    in_specs = (
        P(None, "ty", "tx"),
        P(),
        P("ty", "tx", None, None, None),
        P(None, "ty", "tx", None),
        P("ty", "tx"),
    )
    out_specs = (P(None, "ty", "tx"), P())
    return jax.shard_map(per_device, mesh=mesh, in_specs=in_specs, out_specs=out_specs, check_vma=False)
```

profile of v0, /device:TPU:66, one launch (start us, length us, event | category | flops | bytes accessed | tf_op | source)
XLA Modules:
  0.0 141.1 jit_solution(12550586230388726187)
XLA Ops:
  0.6 0.0 copy-start
  0.6 0.0 copy-start.1
  1.5 0.1 add_and_fusion.odd
  1.5 1.7 %copy-done.2 = f32[2,512,512]{2,1,0:T(8,128)S(1)} copy-done((f32[2,512,512]{2,1,0:T(8,128)S(1)}, f32[2,512,512]{2,1,0:T(8,128)}, u32[]{:S(2)}) %copy-start.2) | copy-done | bytes 2097176
  3.2 0.7 copy-done.8
  3.9 0.7 edges.1
  4.6 2.1 %collective-permute-start = (f32[2,520,128]{2,1,0:T(8,128)S(1)}, f32[2,520,128]{2,1,0:T(8,128)S(1)}, u32[]{:S(2)}, u32[]{:S(2)}) collective-permute-start(f32[2,520,128]{2,1,0:T(8,128)S(1)} %get-tuple-element.28), channel_id=1, source_target_pairs={{1,2},{2,1},{3,4},{4,3},{5,6},{6,5},{7,8},{8,7},{9,10},{10,9},{11,... | collective-permute-start | bytes 1597448 | tf_op jit(solution)/shard_map/ppermute | solution.py:435
  6.7 2.0 %collective-permute-start.1 = (f32[2,520,128]{2,1,0:T(8,128)S(1)}, f32[2,520,128]{2,1,0:T(8,128)S(1)}, u32[]{:S(2)}, u32[]{:S(2)}) collective-permute-start(f32[2,520,128]{2,1,0:T(8,128)S(1)} %get-tuple-element.29), channel_id=1, source_target_pairs={{0,1},{1,0},{2,3},{3,2},{4,5},{5,4},{6,7},{7,6},{8,9},{9,8},{10,11... | collective-permute-start | bytes 1597448 | tf_op jit(solution)/shard_map/ppermute | solution.py:435
  8.7 0.7 collective-permute-start.4
  9.4 3.0 %collective-permute-start.5 = (f32[2,128,512]{2,1,0:T(8,128)S(1)}, f32[2,128,512]{2,1,0:T(8,128)S(1)}, u32[]{:S(2)}, u32[]{:S(2)}) collective-permute-start(f32[2,128,512]{2,1,0:T(8,128)S(1)} %get-tuple-element.34), channel_id=1, source_target_pairs={{0,16},{16,0},{32,48},{48,32},{64,80},{80,64},{96,112},{112,96},{1... | collective-permute-start | bytes 1572872 | tf_op jit(solution)/shard_map/ppermute | solution.py:435
  12.4 1.6 %copy-done.5 = f32[1,1,8,256,256]{4,3,2,1,0:T(8,128)S(1)} copy-done((f32[1,1,8,256,256]{4,3,2,1,0:T(8,128)S(1)}, f32[1,1,8,256,256]{4,3,2,1,0:T(8,128)}, u32[]{:S(2)}) %copy-start.5) | copy-done | bytes 2097176
  14.0 1.0 copy-done.6
  15.0 1.0 copy-done.7
  16.0 1.3 fold.1.folded
  17.4 1.3 core_slots.1
  18.7 13.2 %collective-permute-done.x_first = f32[2,520,128]{2,1,0:T(8,128)S(1)} collective-permute-done((f32[2,520,128]{2,1,0:T(8,128)S(1)}, f32[2,520,128]{2,1,0:T(8,128)S(1)}, u32[]{:S(2)}, u32[]{:S(2)}) %collective-permute-start) | collective-permute-done | bytes 532512 | tf_op jit(solution)/shard_map/ppermute | solution.py:435
  31.8 0.3 collective-permute-done.1.x_second
  32.1 0.6 corners.1
  32.7 0.7 collective-permute-start.2
  33.4 3.0 %collective-permute-start.3 = (f32[2,2,144,128]{3,2,1,0:T(8,128)S(1)}, f32[2,2,144,128]{3,2,1,0:T(8,128)S(1)}, u32[]{:S(2)}, u32[]{:S(2)}) collective-permute-start(f32[2,2,144,128]{3,2,1,0:T(8,128)S(1)} %get-tuple-element.32), channel_id=1, source_target_pairs={{0,16},{16,0},{32,48},{48,32},{64,80},{80,64},{96,112},{112,96},{1... | collective-permute-start | bytes 884744 | tf_op jit(solution)/shard_map/ppermute | solution.py:435
  36.4 3.8 %column_slots.1 = (f32[2,6,768,128]{3,2,1,0:T(8,128)S(1)}, f32[2,6,768,128]{3,2,1,0:T(8,128)S(1)}, f32[3,2,256,128]{3,2,1,0:T(8,128)S(1)}) custom-call(s32[2]{0:T(128)S(1)} %add_and_fusion.odd, s32[2,8]{1,0:T(2,128)S(1)} %bitcast.17, s32[1]{0:T(128)} %bitcast.10.count, ...), custom_call_target="tpu_custom_call", output_to_operand_aliasing={{0}: (9, {}), {1}: (10, {}), {2}: (11, {})} | custom-call | bytes 16777216 | tf_op jit(solution)/shard_map/column_slots/pallas_call | solution.py:538
  40.2 0.0 collective-permute-done.4.y_first
  40.3 0.0 collective-permute-done.5.y_second
  40.3 4.0 %row_slots.1 = (f32[2,6,768,128]{3,2,1,0:T(8,128)S(1)}, f32[2,6,768,128]{3,2,1,0:T(8,128)S(1)}, f32[3,2,256,128]{3,2,1,0:T(8,128)S(1)}) custom-call(s32[2]{0:T(128)S(1)} %add_and_fusion.odd, s32[2,8]{1,0:T(2,128)S(1)} %bitcast.18, s32[1]{0:T(128)} %bitcast.11.count, ...), custom_call_target="tpu_custom_call", output_to_operand_aliasing={{0}: (9, {}), {1}: (10, {}), {2}: (11, {})} | custom-call | bytes 8388608 | tf_op jit(solution)/shard_map/row_slots/pallas_call | solution.py:549
  44.3 0.0 collective-permute-done.2.corner_first
  44.3 0.0 collective-permute-done.3.corner_second
  44.3 3.8 %outer_slots.1 = (f32[2,6,128,128]{3,2,1,0:T(8,128)}, f32[2,6,128,128]{3,2,1,0:T(8,128)}, f32[2,512,128]{2,1,0:T(8,128)}, f32[2,512,128]{2,1,0:T(8,128)}, f32[2,...) custom-call(s32[2]{0:T(128)S(1)} %add_and_fusion.odd, ...), custom_call_target="tpu_custom_call", output_to_operand_aliasing={{7}: (11, {}), {8}: (12, {}), {9}: (13, {})} | custom-call | bytes 16777216 | tf_op jit(solution)/shard_map/outer_slots/pallas_call | solution.py:562
  48.1 0.7 collective-permute-start.6
  48.8 24.6 %all-to-all-start = ((f32[32,6,8,128]{3,2,1,0:T(8,128)}), f32[32,6,8,128]{3,2,1,0:T(8,128)S(1)}, u32[]{:S(2)}, u32[]{:S(2)}) async-start(f32[32,6,8,128]{3,2,1,0:T(8,128)} %get-tuple-element.50), calls=%async_computation | async-start | bytes 1572864 | tf_op jit(solution)/shard_map/all_to_all | solution.py:461
  73.5 0.2 collective-permute-start.7
  73.7 3.0 %weights.1.scale.after = f32[4,512,128]{2,1,0:T(8,128)S(1)} custom-call(f32[9,8,128]{2,1,0:T(8,128)S(1)} %get-tuple-element.47.numbers, f32[2,256,256]{2,1,0:T(8,128)} %probe.11), custom_call_target="tpu_custom_call" | custom-call | bytes 8388608 | tf_op jit(solution)/shard_map/weights/pallas_call | solution.py:580
  76.8 14.2 %all-to-all-done.parts = f32[32,6,8,128]{3,2,1,0:T(8,128)S(1)} async-done(((f32[32,6,8,128]{3,2,1,0:T(8,128)}), f32[32,6,8,128]{3,2,1,0:T(8,128)S(1)}, u32[]{:S(2)}, u32[]{:S(2)}) %all-to-all-start) | async-done | bytes 786464 | tf_op jit(solution)/shard_map/all_to_all | solution.py:461
  90.9 0.0 collective-permute-done.6.y_first.later.low_first.high_first
  90.9 0.7 plane_sum.1
  91.7 9.2 %all-to-all-start.1 = ((f32[8,6,8,128]{3,2,1,0:T(8,128)}), f32[8,6,8,128]{3,2,1,0:T(8,128)S(1)}, u32[]{:S(2)}, u32[]{:S(2)}) async-start(f32[8,6,8,128]{3,2,1,0:T(8,128)} %plane_sum.1), calls=%async_computation.1 | async-start | bytes 393216 | tf_op jit(solution)/shard_map/all_to_all | solution.py:461
  100.9 0.0 collective-permute-done.7.y_second.low_second.high_second
  100.9 6.9 %all-to-all-done.1.after.parts = f32[8,6,8,128]{3,2,1,0:T(8,128)S(1)} async-done(((f32[8,6,8,128]{3,2,1,0:T(8,128)}), f32[8,6,8,128]{3,2,1,0:T(8,128)S(1)}, u32[]{:S(2)}, u32[]{:S(2)}) %all-to-all-start.1) | async-done | bytes 196640 | tf_op jit(solution)/shard_map/all_to_all | solution.py:461
  107.8 2.3 %sides.1 = (f32[2,512,128]{2,1,0:T(8,128)}, f32[2,512,128]{2,1,0:T(8,128)}, f32[8,128]{1,0:T(8,128)S(1)}) custom-call(s32[2]{0:T(128)S(1)} %add_and_fusion.odd, f32[2,512,128]{2,1,0:T(8,128)} %get-tuple-element.48.own_low, f32[2,512,128]{2,1,0:T(8,128)} %get-tuple-element.49.own_high, ...), custom_call_target="tpu_custom_call" | custom-call | bytes 16777216 | tf_op jit(solution)/shard_map/sides/pallas_call | solution.py:608
  110.1 3.7 %collective-permute-start.8 = (f32[2,512,128]{2,1,0:T(8,128)}, f32[2,512,128]{2,1,0:T(8,128)}, u32[]{:S(2)}, u32[]{:S(2)}) collective-permute-start(f32[2,512,128]{2,1,0:T(8,128)} %get-tuple-element.51), channel_id=1, source_target_pairs={{1,2},{2,1},{3,4},{4,3},{5,6},{6,5},{7,8},{8,7},{9,10},{10,9},{11,... | collective-permute-start | bytes 1572872 | tf_op jit(solution)/shard_map/ppermute | solution.py:435
  113.9 3.9 %collective-permute-start.9 = (f32[2,512,128]{2,1,0:T(8,128)}, f32[2,512,128]{2,1,0:T(8,128)}, u32[]{:S(2)}, u32[]{:S(2)}) collective-permute-start(f32[2,512,128]{2,1,0:T(8,128)} %get-tuple-element.52), channel_id=1, source_target_pairs={{0,1},{1,0},{2,3},{3,2},{4,5},{5,4},{6,7},{7,6},{8,9},{9,8},{10,11... | collective-permute-start | bytes 1572872 | tf_op jit(solution)/shard_map/ppermute | solution.py:435
  117.8 1.9 %probe_rows.1 = f32[32,4,8,128]{3,2,1,0:T(8,128)} custom-call(s32[1]{0:T(128)} %bitcast.5.index, f32[8,6,8,128]{3,2,1,0:T(8,128)S(1)} %all-to-all-done.1.after.parts, f32[2,256,256]{2,1,0:T(8,128)} %probe.11, f32[8,128]{1,0:T(8,128)S(1)} %get-tuple-element.53.after), custom_call_target="tpu_custom_call" | custom-call | bytes 2097152 | tf_op jit(solution)/shard_map/probe_rows/pallas_call | solution.py:620
  119.7 4.2 %all-to-all-start.2 = ((f32[32,4,8,128]{3,2,1,0:T(8,128)}), f32[32,4,8,128]{3,2,1,0:T(8,128)S(1)}, u32[]{:S(2)}, u32[]{:S(2)}) async-start(f32[32,4,8,128]{3,2,1,0:T(8,128)} %probe_rows.1), calls=%async_computation.2 | async-start | bytes 1048576 | tf_op jit(solution)/shard_map/all_to_all | solution.py:461
  123.9 4.3 %update.1.before = f32[2,512,512]{2,1,0:T(8,128)} custom-call(s32[2]{0:T(128)S(1)} %add_and_fusion.odd, f32[2,512,512]{2,1,0:T(8,128)} %tile_ref.5, f32[2,4,512,128]{3,2,1,0:T(8,128)} %get-tuple-element.44.grad, f32[2,6,128,128]{3,2,1,0:T(8,128)S(1)} %collective-permute-done.6.y_first.later.low_first.high_first, ...), custom_call_target="tpu_custom_call" | custom-call | bytes 8388608 | tf_op jit(solution)/shard_map/update/pallas_call | solution.py:641
  128.2 4.8 %all-to-all-done.2.pieces = f32[32,4,8,128]{3,2,1,0:T(8,128)S(1)} async-done(((f32[32,4,8,128]{3,2,1,0:T(8,128)}), f32[32,4,8,128]{3,2,1,0:T(8,128)S(1)}, u32[]{:S(2)}, u32[]{:S(2)}) %all-to-all-start.2) | async-done | bytes 524320 | tf_op jit(solution)/shard_map/all_to_all | solution.py:461
  133.0 0.8 join.1
  133.8 0.0 collective-permute-done.8.x_first
  133.8 4.8 %collective-permute-done.9.x_second = f32[2,512,128]{2,1,0:T(8,128)} collective-permute-done((f32[2,512,128]{2,1,0:T(8,128)}, f32[2,512,128]{2,1,0:T(8,128)}, u32[]{:S(2)}, u32[]{:S(2)}) %collective-permute-start.9) | collective-permute-done | bytes 524320 | tf_op jit(solution)/shard_map/ppermute | solution.py:435
  138.7 2.4 %columns.1 = f32[2,512,512]{2,1,0:T(8,128)} custom-call(s32[2]{0:T(128)S(1)} %add_and_fusion.odd, f32[2,512,512]{2,1,0:T(8,128)} %update.1.before, f32[2,512,128]{2,1,0:T(8,128)} %collective-permute-done.8.x_first, f32[2,512,128]{2,1,0:T(8,128)} %collective-permute-done.9.x_second, f32[4,512,128]{2,1,0:T(8,128)S(1)} %weights.1.scale.after), custom_call_target="tpu_custom_call", output_to_operand_aliasing={{}: (1, {})} | custom-call | tf_op jit(solution)/shard_map/columns/pallas_call | solution.py:655
  (13 shorter events, 0.0 us)
Async XLA Ops:
  0.6 16.7 %copy-start = (bf16[4,768,256]{2,1,0:T(8,128)(2,1)S(1)}, bf16[4,768,256]{2,1,0:T(8,128)(2,1)}, u32[]{:S(2)}) copy-start(bf16[4,768,256]{2,1,0:T(8,128)(2,1)} %constant.24.clone.right) | copy-start | bytes 4718596
  0.6 16.7 %copy-start.1 = (bf16[4,256,768]{2,1,0:T(8,128)(2,1)S(1)}, bf16[4,256,768]{2,1,0:T(8,128)(2,1)}, u32[]{:S(2)}) copy-start(bf16[4,256,768]{2,1,0:T(8,128)(2,1)} %constant.23.clone.left) | copy-start | bytes 4718596
  1.5 1.7 %copy-start.2 = (f32[2,512,512]{2,1,0:T(8,128)S(1)}, f32[2,512,512]{2,1,0:T(8,128)}, u32[]{:S(2)}) copy-start(f32[2,512,512]{2,1,0:T(8,128)} %tile_ref.5) | copy-start | bytes 6291460
  3.2 0.7 copy-start.8
  3.9 13.5 %copy-start.3 = (f32[2,512,512]{2,1,0:T(8,128)S(1)}, f32[2,512,512]{2,1,0:T(8,128)}, u32[]{:S(2)}) copy-start(f32[2,512,512]{2,1,0:T(8,128)} %tile_ref.5) | copy-start | bytes 6291460
  3.9 13.5 %copy-start.4 = (f32[2,256,256]{2,1,0:T(8,128)S(1)}, f32[2,256,256]{2,1,0:T(8,128)}, u32[]{:S(2)}) copy-start(f32[2,256,256]{2,1,0:T(8,128)} %probe.11) | copy-start | bytes 1572868
  4.6 27.3 %collective-permute-start = (f32[2,520,128]{2,1,0:T(8,128)S(1)}, f32[2,520,128]{2,1,0:T(8,128)S(1)}, u32[]{:S(2)}, u32[]{:S(2)}) collective-permute-start(f32[2,520,128]{2,1,0:T(8,128)S(1)} %get-tuple-element.28), channel_id=1, source_target_pairs={{1,2},{2,1},{3,4},{4,3},{5,6},{6,5},{7,8},{8,7},{9,10},{10,9},{11,... | collective-permute-start | bytes 1597448 | tf_op jit(solution)/shard_map/ppermute | solution.py:435
  6.7 25.4 %collective-permute-start.1 = (f32[2,520,128]{2,1,0:T(8,128)S(1)}, f32[2,520,128]{2,1,0:T(8,128)S(1)}, u32[]{:S(2)}, u32[]{:S(2)}) collective-permute-start(f32[2,520,128]{2,1,0:T(8,128)S(1)} %get-tuple-element.29), channel_id=1, source_target_pairs={{0,1},{1,0},{2,3},{3,2},{4,5},{5,4},{6,7},{7,6},{8,9},{9,8},{10,11... | collective-permute-start | bytes 1597448 | tf_op jit(solution)/shard_map/ppermute | solution.py:435
  8.7 31.5 %collective-permute-start.4 = (f32[2,128,512]{2,1,0:T(8,128)S(1)}, f32[2,128,512]{2,1,0:T(8,128)S(1)}, u32[]{:S(2)}, u32[]{:S(2)}) collective-permute-start(f32[2,128,512]{2,1,0:T(8,128)S(1)} %get-tuple-element.33), channel_id=1, source_target_pairs={{16,32},{32,16},{48,64},{64,48},{80,96},{96,80},{112,128},{128,112... | collective-permute-start | bytes 1572872 | tf_op jit(solution)/shard_map/ppermute | solution.py:435
  9.4 30.8 %collective-permute-start.5 = (f32[2,128,512]{2,1,0:T(8,128)S(1)}, f32[2,128,512]{2,1,0:T(8,128)S(1)}, u32[]{:S(2)}, u32[]{:S(2)}) collective-permute-start(f32[2,128,512]{2,1,0:T(8,128)S(1)} %get-tuple-element.34), channel_id=1, source_target_pairs={{0,16},{16,0},{32,48},{48,32},{64,80},{80,64},{96,112},{112,96},{1... | collective-permute-start | bytes 1572872 | tf_op jit(solution)/shard_map/ppermute | solution.py:435
  12.4 1.6 %copy-start.5 = (f32[1,1,8,256,256]{4,3,2,1,0:T(8,128)S(1)}, f32[1,1,8,256,256]{4,3,2,1,0:T(8,128)}, u32[]{:S(2)}) copy-start(f32[1,1,8,256,256]{4,3,2,1,0:T(8,128)} %param.11) | copy-start | bytes 6291460
  14.0 1.0 copy-start.6
  15.0 1.0 copy-start.7
  16.0 1.4 copy-start.9
  32.7 11.6 %collective-permute-start.2 = (f32[2,2,144,128]{3,2,1,0:T(8,128)S(1)}, f32[2,2,144,128]{3,2,1,0:T(8,128)S(1)}, u32[]{:S(2)}, u32[]{:S(2)}) collective-permute-start(f32[2,2,144,128]{3,2,1,0:T(8,128)S(1)} %get-tuple-element.31), channel_id=1, source_target_pairs={{16,32},{32,16},{48,64},{64,48},{80,96},{96,80},{112,128},{128,112... | collective-permute-start | bytes 884744 | tf_op jit(solution)/shard_map/ppermute | solution.py:435
  33.4 10.9 %collective-permute-start.3 = (f32[2,2,144,128]{3,2,1,0:T(8,128)S(1)}, f32[2,2,144,128]{3,2,1,0:T(8,128)S(1)}, u32[]{:S(2)}, u32[]{:S(2)}) collective-permute-start(f32[2,2,144,128]{3,2,1,0:T(8,128)S(1)} %get-tuple-element.32), channel_id=1, source_target_pairs={{0,16},{16,0},{32,48},{48,32},{64,80},{80,64},{96,112},{112,96},{1... | collective-permute-start | bytes 884744 | tf_op jit(solution)/shard_map/ppermute | solution.py:435
  48.1 42.8 %collective-permute-start.6 = (f32[2,6,128,128]{3,2,1,0:T(8,128)}, f32[2,6,128,128]{3,2,1,0:T(8,128)S(1)}, u32[]{:S(2)}, u32[]{:S(2)}) collective-permute-start(f32[2,6,128,128]{3,2,1,0:T(8,128)} %get-tuple-element.45), channel_id=1, source_target_pairs={{16,32},{32,16},{48,64},{64,48},{80,96},{96,80},{112,128},{128,112... | collective-permute-start | bytes 2359304 | tf_op jit(solution)/shard_map/ppermute | solution.py:435
  48.8 42.1 %all-to-all-start = ((f32[32,6,8,128]{3,2,1,0:T(8,128)}), f32[32,6,8,128]{3,2,1,0:T(8,128)S(1)}, u32[]{:S(2)}, u32[]{:S(2)}) async-start(f32[32,6,8,128]{3,2,1,0:T(8,128)} %get-tuple-element.50), calls=%async_computation | async-start | bytes 1572864 | tf_op jit(solution)/shard_map/all_to_all | solution.py:461
  73.5 27.4 %collective-permute-start.7 = (f32[2,6,128,128]{3,2,1,0:T(8,128)}, f32[2,6,128,128]{3,2,1,0:T(8,128)S(1)}, u32[]{:S(2)}, u32[]{:S(2)}) collective-permute-start(f32[2,6,128,128]{3,2,1,0:T(8,128)} %get-tuple-element.46), channel_id=1, source_target_pairs={{0,16},{16,0},{32,48},{48,32},{64,80},{80,64},{96,112},{112,96},{1... | collective-permute-start | bytes 2359304 | tf_op jit(solution)/shard_map/ppermute | solution.py:435
  91.7 16.1 %all-to-all-start.1 = ((f32[8,6,8,128]{3,2,1,0:T(8,128)}), f32[8,6,8,128]{3,2,1,0:T(8,128)S(1)}, u32[]{:S(2)}, u32[]{:S(2)}) async-start(f32[8,6,8,128]{3,2,1,0:T(8,128)} %plane_sum.1), calls=%async_computation.1 | async-start | bytes 393216 | tf_op jit(solution)/shard_map/all_to_all | solution.py:461
  110.1 23.7 %collective-permute-start.8 = (f32[2,512,128]{2,1,0:T(8,128)}, f32[2,512,128]{2,1,0:T(8,128)}, u32[]{:S(2)}, u32[]{:S(2)}) collective-permute-start(f32[2,512,128]{2,1,0:T(8,128)} %get-tuple-element.51), channel_id=1, source_target_pairs={{1,2},{2,1},{3,4},{4,3},{5,6},{6,5},{7,8},{8,7},{9,10},{10,9},{11,... | collective-permute-start | bytes 1572872 | tf_op jit(solution)/shard_map/ppermute | solution.py:435
  113.9 24.8 %collective-permute-start.9 = (f32[2,512,128]{2,1,0:T(8,128)}, f32[2,512,128]{2,1,0:T(8,128)}, u32[]{:S(2)}, u32[]{:S(2)}) collective-permute-start(f32[2,512,128]{2,1,0:T(8,128)} %get-tuple-element.52), channel_id=1, source_target_pairs={{0,1},{1,0},{2,3},{3,2},{4,5},{5,4},{6,7},{7,6},{8,9},{9,8},{10,11... | collective-permute-start | bytes 1572872 | tf_op jit(solution)/shard_map/ppermute | solution.py:435
  119.7 13.3 %all-to-all-start.2 = ((f32[32,4,8,128]{3,2,1,0:T(8,128)}), f32[32,4,8,128]{3,2,1,0:T(8,128)S(1)}, u32[]{:S(2)}, u32[]{:S(2)}) async-start(f32[32,4,8,128]{3,2,1,0:T(8,128)} %probe_rows.1), calls=%async_computation.2 | async-start | bytes 1048576 | tf_op jit(solution)/shard_map/all_to_all | solution.py:461
where the time goes:
time: 143 us; the launch traced here: 141 us
  starting transfers between devices  58.2 us (41%)
  waiting for transfers between devices  44.1 us (31%)
  Pallas kernels  31.1 us (22%)
  local copies, waits for them, and re-layouts  5.94 us (4%)
  between operations  1.65 us (1%)
    all_to_all x3, starting transfers between devices, trade(): lax.all_to_all(pieces, ('ty', 'tx'), 0, 0, axis_index_groups=groups, tile...  38.1 us
    all_to_all x3, waiting for transfers between devices, trade(): lax.all_to_all(pieces, ('ty', 'tx'), 0, 0, axis_index_groups=groups, tile...  25.9 us
    ppermute x5, waiting for transfers between devices, swap(): lax.ppermute(first, axis, across)  13.2 us
    ppermute x5, starting transfers between devices, swap(): lax.ppermute(second, axis, [(index, index ^ 1) for index in range(count)])  12.2 us
    ppermute x5, starting transfers between devices, swap(): lax.ppermute(first, axis, across)  7.95 us
    unnamed x20, local copies, waits for them, and re-layouts  5.94 us
    ppermute x5, waiting for transfers between devices, swap(): lax.ppermute(second, axis, [(index, index ^ 1) for index in range(count)])  5.1 us
    pallas_call x1, Pallas kernels, per_device(): pl.pallas_call(update_kernel, out_shape=jax.ShapeDtypeStruct(object_field...  4.29 us
  transfers between devices with their start and end apart: 13, of which 6 were waited for; matrix products, arithmetic and copies ran while one was open for 0% of the time, Pallas kernels for 15%

commit v1 on v0

--- a/solution.py
+++ b/solution.py
@@ -340,7 +340,7 @@
         copy.wait()
 
 
-def sides_kernel(odd, own_low, own_high, low_first, low_second, high_first, high_second, after, first, second, token):
+def sides_kernel(odd, own_low, own_high, low_first, low_second, high_first, high_second, after, first, second):
     half = LANES
     side = own_low.shape[1]
     odd_y, odd_x = odd[0] == 1, odd[1] == 1
@@ -356,7 +356,6 @@
             values.append(value)
         first[:, rows, :] = jnp.where(odd_x, values[1], values[0])
         second[:, rows, :] = jnp.where(odd_x, values[0], values[1])
-    token[...] = jnp.zeros_like(token)
 
 
 def weight_kernel(numbers, probe, scale, power, weight):
@@ -402,17 +401,30 @@
             out[plane, rows, :] = tile_ref[plane, rows, :] - value * scale[0, rows, :]
 
 
-def column_kernel(odd, before, x_first, x_second, scale, out):
-    use_first = odd[1] == pl.program_id(0)
-    for plane in range(2):
-        out[plane] = before[plane] - jnp.where(use_first, x_first[plane], x_second[plane]) * scale[0]
-
-
-def plane_kernel(parts, after, later, out):
+def column_kernel(odd, x_first, x_second, scale, whole, out, columns, sems):
+    half = LANES
+    far = out.shape[2] - half
+    odd_x = odd[1] == 1
+    places = [out.at[:, :, start : start + half] for start in (0, far)]
+    loads = [pltpu.make_async_copy(place, columns.at[index], sems.at[index]) for index, place in enumerate(places)]
+    stores = [pltpu.make_async_copy(columns.at[index], place, sems.at[2 + index]) for index, place in enumerate(places)]
+    for load in loads:
+        load.start()
+    for index, (tile, even_ref, odd_ref) in enumerate(((0, x_first, x_second), (scale.shape[0] - 1, x_second, x_first))):
+        loads[index].wait()
+        for plane in range(2):
+            strip = jnp.where(odd_x, odd_ref[plane], even_ref[plane])
+            columns[index, plane] = columns[index, plane] - strip * scale[tile]
+        stores[index].start()
+    for store in stores:
+        store.wait()
+
+
+def plane_kernel(parts, after, out):
     out[...] = jnp.broadcast_to(jnp.sum(parts[...], axis=0)[None], out.shape)
 
 
-def probe_kernel(index, parts, probe, after, out):
+def probe_kernel(index, parts, probe, out):
     total = jnp.sum(parts[...], axis=0)
     rows = pl.ds(pl.multiple_of(index[0] * 8, 8), 8)
     for tile in range(2):
@@ -594,23 +606,23 @@
         parts = pl.pallas_call(
             plane_kernel,
             out_shape=pltpu.HBM((len(lines[0]), 6, 8, LANES), F32),
-            in_specs=[VMEM, HBM, HBM],
+            in_specs=[VMEM, HBM],
             out_specs=VMEM,
             compiler_params=params(6),
             cost_estimate=cost(2),
             name="plane_sum",
-        )(parts, scale, margin_first)
+        )(parts, scale)
         parts = trade(parts, lines)
         strip = pltpu.HBM((2, side, LANES), F32)
         whole = pl.BlockSpec((2, side, LANES), lambda index: (0, 0, 0))
         first_tile = pl.BlockSpec((2, 1, half, LANES), lambda index: (0, 0, 0, 0))
         last_tile = pl.BlockSpec((2, 1, half, LANES), lambda index: (0, tiles + 1, 0, 0))
-        *margins, token = pl.pallas_call(
+        margins = pl.pallas_call(
             sides_kernel,
-            out_shape=(strip, strip, jax.ShapeDtypeStruct((8, LANES), F32)),
+            out_shape=(strip, strip),
             grid=(1,),
             in_specs=[SMEM, whole, whole, first_tile, first_tile, last_tile, last_tile, HBM],
-            out_specs=(whole, whole, pl.BlockSpec((8, LANES), lambda index: (0, 0))),
+            out_specs=(whole, whole),
             compiler_params=params(8),
             cost_estimate=cost(16),
             name="sides",
@@ -620,12 +632,12 @@
         pieces = pl.pallas_call(
             probe_kernel,
             out_shape=pltpu.HBM((members, 4, 8, LANES), F32),
-            in_specs=[SMEM, VMEM, VMEM, HBM],
+            in_specs=[SMEM, VMEM, VMEM],
             out_specs=VMEM,
             compiler_params=params(6),
             cost_estimate=cost(2),
             name="probe_rows",
-        )(piece, parts, keep(probe), token)
+        )(piece, parts, keep(probe))
         probe_new = pl.pallas_call(
             join_kernel,
             out_shape=jax.ShapeDtypeStruct(probe.shape, F32),
@@ -640,7 +652,7 @@
         flat = pl.BlockSpec((2, 1, half, LANES), lambda index: (0, index + 1, 0, 0))
         object_new = pl.pallas_call(
             update_kernel,
-            out_shape=jax.ShapeDtypeStruct(object_field.shape, F32),
+            out_shape=pltpu.HBM(object_field.shape, F32),
             grid=(tiles,),
             in_specs=[
                 SMEM, column, pl.BlockSpec((2, 1, side, LANES), lambda index: (0, index, 0, 0)), flat, flat,
@@ -651,17 +663,16 @@
             cost_estimate=cost(8),
             name="update",
         )(odd, keep(object_field), keep(middle), margin_first, margin_second, scale)
-        ends = pl.BlockSpec((2, side, LANES), lambda index: (0, 0, index * (tiles - 1)))
         object_new = pl.pallas_call(
             column_kernel,
-            out_shape=jax.ShapeDtypeStruct(object_field.shape, F32),
-            grid=(2,),
-            in_specs=[SMEM, ends, whole, whole, pl.BlockSpec((1, side, LANES), lambda index: (index * (tiles - 1), 0, 0))],
-            out_specs=ends,
-            input_output_aliases={1: 0},
+            out_shape=pltpu.HBM(object_field.shape, F32),
+            in_specs=[SMEM] + [VMEM] * 3 + [HBM],
+            out_specs=HBM,
+            scratch_shapes=[pltpu.VMEM((2, 2, side, LANES), F32), pltpu.SemaphoreType.DMA((4,))],
+            input_output_aliases={4: 0},
             compiler_params=params(8),
             name="columns",
-        )(odd, object_new, x_first, x_second, scale)
+        )(odd, x_first, x_second, scale, object_new)
         return (object_new, probe_new)
 
     in_specs = (

time: 143 us -> 136 us (0.951)
  the two profiles are of different devices: /device:TPU:66 before, /device:TPU:1 now
where the time goes in v1:
time: 136 us; the launch traced here: 134 us
  starting transfers between devices  51.7 us (38%)
  Pallas kernels  40.6 us (30%)
  waiting for transfers between devices  33.7 us (25%)
  local copies, waits for them, and re-layouts  5.93 us (4%)
  between operations  1.85 us (1%)
    all_to_all x3, starting transfers between devices, trade(): lax.all_to_all(pieces, ('ty', 'tx'), 0, 0, axis_index_groups=groups, tile...  29.6 us
    all_to_all x3, waiting for transfers between devices, trade(): lax.all_to_all(pieces, ('ty', 'tx'), 0, 0, axis_index_groups=groups, tile...  26.6 us
    ppermute x5, starting transfers between devices, swap(): lax.ppermute(first, axis, across)  14.7 us
    ppermute x5, starting transfers between devices, swap(): lax.ppermute(second, axis, [(index, index ^ 1) for index in range(count)])  7.39 us
    ppermute x5, waiting for transfers between devices, swap(): lax.ppermute(second, axis, [(index, index ^ 1) for index in range(count)])  7.1 us
    pallas_call x1, Pallas kernels, per_device(): pl.pallas_call(outer_kernel, out_shape=(margin, margin, column, column, p...  6.99 us
    unnamed x20, local copies, waits for them, and re-layouts  5.93 us
    pallas_call x1, Pallas kernels, per_device(): pl.pallas_call(core_kernel, out_shape=state + (jax.ShapeDtypeStruct((8, L...  4.45 us
  transfers between devices with their start and end apart: 13, of which 4 were waited for; matrix products, arithmetic and copies ran while one was open for 0% of the time, Pallas kernels for 20%

profile of v1, /device:TPU:1, one launch (start us, length us, event | category | flops | bytes accessed | tf_op | source)
XLA Modules:
  0.0 133.8 jit_solution(17893185562018870405)
XLA Ops:
  0.6 0.0 copy-start
  0.6 0.0 copy-start.1
  1.5 0.1 add_and_fusion.odd
  1.5 1.7 %copy-done.2 = f32[2,512,512]{2,1,0:T(8,128)S(1)} copy-done((f32[2,512,512]{2,1,0:T(8,128)S(1)}, f32[2,512,512]{2,1,0:T(8,128)}, u32[]{:S(2)}) %copy-start.2) | copy-done | bytes 2097176
  3.2 0.7 copy-done.8
  3.9 0.7 edges.1
  4.6 0.8 collective-permute-start
  5.4 5.4 %collective-permute-start.1 = (f32[2,520,128]{2,1,0:T(8,128)S(1)}, f32[2,520,128]{2,1,0:T(8,128)S(1)}, u32[]{:S(2)}, u32[]{:S(2)}) collective-permute-start(f32[2,520,128]{2,1,0:T(8,128)S(1)} %get-tuple-element.28), channel_id=1, source_target_pairs={{0,1},{1,0},{2,3},{3,2},{4,5},{5,4},{6,7},{7,6},{8,9},{9,8},{10,11... | collective-permute-start | bytes 1597448 | tf_op jit(solution)/shard_map/ppermute | solution.py:447
  10.8 4.3 %collective-permute-start.4 = (f32[2,128,512]{2,1,0:T(8,128)S(1)}, f32[2,128,512]{2,1,0:T(8,128)S(1)}, u32[]{:S(2)}, u32[]{:S(2)}) collective-permute-start(f32[2,128,512]{2,1,0:T(8,128)S(1)} %get-tuple-element.32), channel_id=1, source_target_pairs={{16,32},{32,16},{48,64},{64,48},{80,96},{96,80},{112,128},{128,112... | collective-permute-start | bytes 1572872 | tf_op jit(solution)/shard_map/ppermute | solution.py:447
  15.1 0.1 collective-permute-start.5
  15.2 0.0 copy-start.5
  15.2 1.6 %copy-done.5 = f32[1,1,8,256,256]{4,3,2,1,0:T(8,128)S(1)} copy-done((f32[1,1,8,256,256]{4,3,2,1,0:T(8,128)S(1)}, f32[1,1,8,256,256]{4,3,2,1,0:T(8,128)}, u32[]{:S(2)}) %copy-start.5) | copy-done | bytes 2097176
  16.8 1.0 copy-done.6
  17.8 1.0 copy-done.7
  18.8 3.4 %fold.1.folded = f32[8,256,256]{2,1,0:T(8,128)S(1)} custom-call(s32[1]{0:T(128)} %bitcast.6.count, f32[8,256,256]{2,1,0:T(8,128)S(1)} %bitcast.13, bf16[256,768]{1,0:T(8,128)(2,1)S(1)} %copy-done.7, bf16[768,256]{1,0:T(8,128)(2,1)S(1)} %copy-done.6), custom_call_target="tpu_custom_call" | custom-call | bytes 6291456 | tf_op jit(solution)/shard_map/fold/pallas_call | solution.py:504
  22.2 4.4 %core_slots.1 = (f32[2,6,768,128]{3,2,1,0:T(8,128)S(1)}, f32[2,6,768,128]{3,2,1,0:T(8,128)S(1)}, f32[3,2,256,128]{3,2,1,0:T(8,128)S(1)}, f32[8,128]{1,0:T(8,128)S(1)}) custom-call(s32[2]{0:T(128)S(1)} %add_and_fusion.odd, s32[2,8]{1,0:T(2,128)S(1)} %bitcast.15, s32[1]{0:T(128)} %bitcast.8.count, f32[2,256,256]{2,1,0:T(8,128)S(1)} %copy-done.4, ...), custom_call_target="tpu_custom_call" | custom-call | bytes 16777216 | tf_op jit(solution)/shard_map/core_slots/pallas_call | solution.py:528
  26.7 0.0 collective-permute-done.x_first
  26.7 7.1 %collective-permute-done.1.x_second = f32[2,520,128]{2,1,0:T(8,128)S(1)} collective-permute-done((f32[2,520,128]{2,1,0:T(8,128)S(1)}, f32[2,520,128]{2,1,0:T(8,128)S(1)}, u32[]{:S(2)}, u32[]{:S(2)}) %collective-permute-start.1) | collective-permute-done | bytes 532512 | tf_op jit(solution)/shard_map/ppermute | solution.py:447
  33.8 0.6 corners.1
  34.4 4.6 %collective-permute-start.2 = (f32[2,2,144,128]{3,2,1,0:T(8,128)S(1)}, f32[2,2,144,128]{3,2,1,0:T(8,128)S(1)}, u32[]{:S(2)}, u32[]{:S(2)}) collective-permute-start(f32[2,2,144,128]{3,2,1,0:T(8,128)S(1)} %get-tuple-element.30), channel_id=1, source_target_pairs={{16,32},{32,16},{48,64},{64,48},{80,96},{96,80},{112,128},{128,112... | collective-permute-start | bytes 884744 | tf_op jit(solution)/shard_map/ppermute | solution.py:447
  39.0 0.1 collective-permute-start.3
  39.1 3.9 %column_slots.1 = (f32[2,6,768,128]{3,2,1,0:T(8,128)S(1)}, f32[2,6,768,128]{3,2,1,0:T(8,128)S(1)}, f32[3,2,256,128]{3,2,1,0:T(8,128)S(1)}) custom-call(s32[2]{0:T(128)S(1)} %add_and_fusion.odd, s32[2,8]{1,0:T(2,128)S(1)} %bitcast.17, s32[1]{0:T(128)} %bitcast.10.count, ...), custom_call_target="tpu_custom_call", output_to_operand_aliasing={{0}: (9, {}), {1}: (10, {}), {2}: (11, {})} | custom-call | bytes 16777216 | tf_op jit(solution)/shard_map/column_slots/pallas_call | solution.py:550
  43.0 0.0 collective-permute-done.5.y_second
  43.0 4.0 %row_slots.1 = (f32[2,6,768,128]{3,2,1,0:T(8,128)S(1)}, f32[2,6,768,128]{3,2,1,0:T(8,128)S(1)}, f32[3,2,256,128]{3,2,1,0:T(8,128)S(1)}) custom-call(s32[2]{0:T(128)S(1)} %add_and_fusion.odd, s32[2,8]{1,0:T(2,128)S(1)} %bitcast.18, s32[1]{0:T(128)} %bitcast.11.count, ...), custom_call_target="tpu_custom_call", output_to_operand_aliasing={{0}: (9, {}), {1}: (10, {}), {2}: (11, {})} | custom-call | bytes 8388608 | tf_op jit(solution)/shard_map/row_slots/pallas_call | solution.py:561
  47.0 0.0 collective-permute-done.2.corner_first
  47.0 0.0 collective-permute-done.3.corner_second
  47.1 7.0 %outer_slots.1 = (f32[2,6,128,128]{3,2,1,0:T(8,128)}, f32[2,6,128,128]{3,2,1,0:T(8,128)}, f32[2,512,128]{2,1,0:T(8,128)}, f32[2,512,128]{2,1,0:T(8,128)}, f32[2,...) custom-call(s32[2]{0:T(128)S(1)} %add_and_fusion.odd, ...), custom_call_target="tpu_custom_call", output_to_operand_aliasing={{7}: (11, {}), {8}: (12, {}), {9}: (13, {})} | custom-call | bytes 16777216 | tf_op jit(solution)/shard_map/outer_slots/pallas_call | solution.py:574
  54.1 14.1 %all-to-all-start = ((f32[32,6,8,128]{3,2,1,0:T(8,128)}), f32[32,6,8,128]{3,2,1,0:T(8,128)S(1)}, u32[]{:S(2)}, u32[]{:S(2)}) async-start(f32[32,6,8,128]{3,2,1,0:T(8,128)} %get-tuple-element.47), calls=%async_computation | async-start | bytes 1572864 | tf_op jit(solution)/shard_map/all_to_all | solution.py:473
  68.1 3.5 %collective-permute-start.6 = (f32[2,6,128,128]{3,2,1,0:T(8,128)}, f32[2,6,128,128]{3,2,1,0:T(8,128)S(1)}, u32[]{:S(2)}, u32[]{:S(2)}) collective-permute-start(f32[2,6,128,128]{3,2,1,0:T(8,128)} %get-tuple-element.45), channel_id=1, source_target_pairs={{16,32},{32,16},{48,64},{64,48},{80,96},{96,80},{112,128},{128,112... | collective-permute-start | bytes 2359304 | tf_op jit(solution)/shard_map/ppermute | solution.py:447
  71.7 0.1 collective-permute-start.7
  71.8 3.1 %weights.1.after.scale = f32[4,512,128]{2,1,0:T(8,128)S(1)} custom-call(f32[9,8,128]{2,1,0:T(8,128)S(1)} %get-tuple-element.48.numbers, f32[2,256,256]{2,1,0:T(8,128)} %probe.11), custom_call_target="tpu_custom_call" | custom-call | bytes 8388608 | tf_op jit(solution)/shard_map/weights/pallas_call | solution.py:592
  74.9 6.9 %all-to-all-done.parts = f32[32,6,8,128]{3,2,1,0:T(8,128)S(1)} async-done(((f32[32,6,8,128]{3,2,1,0:T(8,128)}), f32[32,6,8,128]{3,2,1,0:T(8,128)S(1)}, u32[]{:S(2)}, u32[]{:S(2)}) %all-to-all-start) | async-done | bytes 786464 | tf_op jit(solution)/shard_map/all_to_all | solution.py:473
  81.8 0.8 plane_sum.1
  82.6 9.8 %all-to-all-start.1 = ((f32[8,6,8,128]{3,2,1,0:T(8,128)}), f32[8,6,8,128]{3,2,1,0:T(8,128)S(1)}, u32[]{:S(2)}, u32[]{:S(2)}) async-start(f32[8,6,8,128]{3,2,1,0:T(8,128)} %plane_sum.1), calls=%async_computation.1 | async-start | bytes 393216 | tf_op jit(solution)/shard_map/all_to_all | solution.py:473
  92.3 0.0 collective-permute-done.6.low_first.high_first.y_first
  92.3 0.0 collective-permute-done.7.low_second.high_second.y_second
  92.3 10.0 %all-to-all-done.1.after.parts = f32[8,6,8,128]{3,2,1,0:T(8,128)S(1)} async-done(((f32[8,6,8,128]{3,2,1,0:T(8,128)}), f32[8,6,8,128]{3,2,1,0:T(8,128)S(1)}, u32[]{:S(2)}, u32[]{:S(2)}) %all-to-all-start.1) | async-done | bytes 196640 | tf_op jit(solution)/shard_map/all_to_all | solution.py:473
  102.3 2.3 %sides.1 = (f32[2,512,128]{2,1,0:T(8,128)}, f32[2,512,128]{2,1,0:T(8,128)}) custom-call(s32[2]{0:T(128)S(1)} %add_and_fusion.odd, f32[2,512,128]{2,1,0:T(8,128)} %get-tuple-element.43.own_low, f32[2,512,128]{2,1,0:T(8,128)} %get-tuple-element.44.own_high, f32[2,6,128,128]{3,2,1,0:T(8,128)S(1)} %collective-permute-done.6.low_first.high_first.y_first, ...), custom_call_target="tpu_custom_call" | custom-call | bytes 16777216 | tf_op jit(solution)/shard_map/sides/pallas_call | solution.py:620
  104.6 1.5 %collective-permute-start.8 = (f32[2,512,128]{2,1,0:T(8,128)}, f32[2,512,128]{2,1,0:T(8,128)}, u32[]{:S(2)}, u32[]{:S(2)}) collective-permute-start(f32[2,512,128]{2,1,0:T(8,128)} %get-tuple-element.49), channel_id=1, source_target_pairs={{1,2},{2,1},{3,4},{4,3},{5,6},{6,5},{7,8},{8,7},{9,10},{10,9},{11,... | collective-permute-start | bytes 1572872 | tf_op jit(solution)/shard_map/ppermute | solution.py:447
  106.1 1.7 %collective-permute-start.9 = (f32[2,512,128]{2,1,0:T(8,128)}, f32[2,512,128]{2,1,0:T(8,128)}, u32[]{:S(2)}, u32[]{:S(2)}) collective-permute-start(f32[2,512,128]{2,1,0:T(8,128)} %get-tuple-element.50), channel_id=1, source_target_pairs={{0,1},{1,0},{2,3},{3,2},{4,5},{5,4},{6,7},{7,6},{8,9},{9,8},{10,11... | collective-permute-start | bytes 1572872 | tf_op jit(solution)/shard_map/ppermute | solution.py:447
  107.8 1.9 %probe_rows.1 = f32[32,4,8,128]{3,2,1,0:T(8,128)} custom-call(s32[1]{0:T(128)} %bitcast.5.index, f32[8,6,8,128]{3,2,1,0:T(8,128)S(1)} %all-to-all-done.1.after.parts, f32[2,256,256]{2,1,0:T(8,128)} %probe.11), custom_call_target="tpu_custom_call" | custom-call | bytes 2097152 | tf_op jit(solution)/shard_map/probe_rows/pallas_call | solution.py:632
  109.7 5.7 %all-to-all-start.2 = ((f32[32,4,8,128]{3,2,1,0:T(8,128)}), f32[32,4,8,128]{3,2,1,0:T(8,128)S(1)}, u32[]{:S(2)}, u32[]{:S(2)}) async-start(f32[32,4,8,128]{3,2,1,0:T(8,128)} %probe_rows.1), calls=%async_computation.2 | async-start | bytes 1048576 | tf_op jit(solution)/shard_map/all_to_all | solution.py:473
  115.5 4.3 %update.1.whole = f32[2,512,512]{2,1,0:T(8,128)} custom-call(s32[2]{0:T(128)S(1)} %add_and_fusion.odd, f32[2,512,512]{2,1,0:T(8,128)} %tile_ref.5, f32[2,4,512,128]{3,2,1,0:T(8,128)} %get-tuple-element.51.grad, f32[2,6,128,128]{3,2,1,0:T(8,128)S(1)} %collective-permute-done.6.low_first.high_first.y_first, ...), custom_call_target="tpu_custom_call" | custom-call | bytes 8388608 | tf_op jit(solution)/shard_map/update/pallas_call | solution.py:653
  119.7 9.7 %all-to-all-done.2.pieces = f32[32,4,8,128]{3,2,1,0:T(8,128)S(1)} async-done(((f32[32,4,8,128]{3,2,1,0:T(8,128)}), f32[32,4,8,128]{3,2,1,0:T(8,128)S(1)}, u32[]{:S(2)}, u32[]{:S(2)}) %all-to-all-start.2) | async-done | bytes 524320 | tf_op jit(solution)/shard_map/all_to_all | solution.py:473
  129.4 0.8 join.1
  130.3 0.0 collective-permute-done.8.x_first
  130.3 0.0 collective-permute-done.9.x_second
  130.3 3.3 %columns.1 = f32[2,512,512]{2,1,0:T(8,128)} custom-call(s32[2]{0:T(128)S(1)} %add_and_fusion.odd, f32[2,512,128]{2,1,0:T(8,128)} %collective-permute-done.8.x_first, f32[2,512,128]{2,1,0:T(8,128)} %collective-permute-done.9.x_second, f32[4,512,128]{2,1,0:T(8,128)S(1)} %weights.1.after.scale, f32[2,512,512]{2,1,0:T(8,128)} %update.1.whole), custom_call_target="tpu_custom_call", output_to_operand_aliasing={{}: (4, {})} | custom-call | tf_op jit(solution)/shard_map/columns/pallas_call | solution.py:666
  (13 shorter events, 0.0 us)
Async XLA Ops:
  0.6 21.6 %copy-start = (bf16[4,768,256]{2,1,0:T(8,128)(2,1)S(1)}, bf16[4,768,256]{2,1,0:T(8,128)(2,1)}, u32[]{:S(2)}) copy-start(bf16[4,768,256]{2,1,0:T(8,128)(2,1)} %constant.24.clone.right) | copy-start | bytes 4718596
  0.6 21.6 %copy-start.1 = (bf16[4,256,768]{2,1,0:T(8,128)(2,1)S(1)}, bf16[4,256,768]{2,1,0:T(8,128)(2,1)}, u32[]{:S(2)}) copy-start(bf16[4,256,768]{2,1,0:T(8,128)(2,1)} %constant.23.clone.left) | copy-start | bytes 4718596
  1.5 1.7 %copy-start.2 = (f32[2,512,512]{2,1,0:T(8,128)S(1)}, f32[2,512,512]{2,1,0:T(8,128)}, u32[]{:S(2)}) copy-start(f32[2,512,512]{2,1,0:T(8,128)} %tile_ref.5) | copy-start | bytes 6291460
  3.2 0.7 copy-start.8
  3.9 18.3 %copy-start.3 = (f32[2,512,512]{2,1,0:T(8,128)S(1)}, f32[2,512,512]{2,1,0:T(8,128)}, u32[]{:S(2)}) copy-start(f32[2,512,512]{2,1,0:T(8,128)} %tile_ref.5) | copy-start | bytes 6291460
  3.9 18.3 %copy-start.4 = (f32[2,256,256]{2,1,0:T(8,128)S(1)}, f32[2,256,256]{2,1,0:T(8,128)}, u32[]{:S(2)}) copy-start(f32[2,256,256]{2,1,0:T(8,128)} %probe.11) | copy-start | bytes 1572868
  4.6 22.1 %collective-permute-start = (f32[2,520,128]{2,1,0:T(8,128)S(1)}, f32[2,520,128]{2,1,0:T(8,128)S(1)}, u32[]{:S(2)}, u32[]{:S(2)}) collective-permute-start(f32[2,520,128]{2,1,0:T(8,128)S(1)} %get-tuple-element.27), channel_id=1, source_target_pairs={{1,2},{2,1},{3,4},{4,3},{5,6},{6,5},{7,8},{8,7},{9,10},{10,9},{11,... | collective-permute-start | bytes 1597448 | tf_op jit(solution)/shard_map/ppermute | solution.py:447
  5.4 28.4 %collective-permute-start.1 = (f32[2,520,128]{2,1,0:T(8,128)S(1)}, f32[2,520,128]{2,1,0:T(8,128)S(1)}, u32[]{:S(2)}, u32[]{:S(2)}) collective-permute-start(f32[2,520,128]{2,1,0:T(8,128)S(1)} %get-tuple-element.28), channel_id=1, source_target_pairs={{0,1},{1,0},{2,3},{3,2},{4,5},{5,4},{6,7},{7,6},{8,9},{9,8},{10,11... | collective-permute-start | bytes 1597448 | tf_op jit(solution)/shard_map/ppermute | solution.py:447
  10.8 32.2 %collective-permute-start.4 = (f32[2,128,512]{2,1,0:T(8,128)S(1)}, f32[2,128,512]{2,1,0:T(8,128)S(1)}, u32[]{:S(2)}, u32[]{:S(2)}) collective-permute-start(f32[2,128,512]{2,1,0:T(8,128)S(1)} %get-tuple-element.32), channel_id=1, source_target_pairs={{16,32},{32,16},{48,64},{64,48},{80,96},{96,80},{112,128},{128,112... | collective-permute-start | bytes 1572872 | tf_op jit(solution)/shard_map/ppermute | solution.py:447
  15.1 27.9 %collective-permute-start.5 = (f32[2,128,512]{2,1,0:T(8,128)S(1)}, f32[2,128,512]{2,1,0:T(8,128)S(1)}, u32[]{:S(2)}, u32[]{:S(2)}) collective-permute-start(f32[2,128,512]{2,1,0:T(8,128)S(1)} %get-tuple-element.33), channel_id=1, source_target_pairs={{0,16},{16,0},{32,48},{48,32},{64,80},{80,64},{96,112},{112,96},{1... | collective-permute-start | bytes 1572872 | tf_op jit(solution)/shard_map/ppermute | solution.py:447
  15.2 1.6 %copy-start.5 = (f32[1,1,8,256,256]{4,3,2,1,0:T(8,128)S(1)}, f32[1,1,8,256,256]{4,3,2,1,0:T(8,128)}, u32[]{:S(2)}) copy-start(f32[1,1,8,256,256]{4,3,2,1,0:T(8,128)} %param.11) | copy-start | bytes 6291460
  16.8 1.0 copy-start.6
  17.8 1.0 copy-start.7
  18.8 3.4 %copy-start.9 = (s32[2,1,1,8]{3,2,1,0:T(1,128)S(1)}, s32[2,1,1,8]{3,2,1,0:T(1,128)}, u32[]{:S(2)}) copy-start(s32[2,1,1,8]{3,2,1,0:T(1,128)} %param.12) | copy-start | bytes 196
  34.4 12.6 %collective-permute-start.2 = (f32[2,2,144,128]{3,2,1,0:T(8,128)S(1)}, f32[2,2,144,128]{3,2,1,0:T(8,128)S(1)}, u32[]{:S(2)}, u32[]{:S(2)}) collective-permute-start(f32[2,2,144,128]{3,2,1,0:T(8,128)S(1)} %get-tuple-element.30), channel_id=1, source_target_pairs={{16,32},{32,16},{48,64},{64,48},{80,96},{96,80},{112,128},{128,112... | collective-permute-start | bytes 884744 | tf_op jit(solution)/shard_map/ppermute | solution.py:447
  39.0 8.1 %collective-permute-start.3 = (f32[2,2,144,128]{3,2,1,0:T(8,128)S(1)}, f32[2,2,144,128]{3,2,1,0:T(8,128)S(1)}, u32[]{:S(2)}, u32[]{:S(2)}) collective-permute-start(f32[2,2,144,128]{3,2,1,0:T(8,128)S(1)} %get-tuple-element.31), channel_id=1, source_target_pairs={{0,16},{16,0},{32,48},{48,32},{64,80},{80,64},{96,112},{112,96},{1... | collective-permute-start | bytes 884744 | tf_op jit(solution)/shard_map/ppermute | solution.py:447
  54.1 27.8 %all-to-all-start = ((f32[32,6,8,128]{3,2,1,0:T(8,128)}), f32[32,6,8,128]{3,2,1,0:T(8,128)S(1)}, u32[]{:S(2)}, u32[]{:S(2)}) async-start(f32[32,6,8,128]{3,2,1,0:T(8,128)} %get-tuple-element.47), calls=%async_computation | async-start | bytes 1572864 | tf_op jit(solution)/shard_map/all_to_all | solution.py:473
  68.1 24.2 %collective-permute-start.6 = (f32[2,6,128,128]{3,2,1,0:T(8,128)}, f32[2,6,128,128]{3,2,1,0:T(8,128)S(1)}, u32[]{:S(2)}, u32[]{:S(2)}) collective-permute-start(f32[2,6,128,128]{3,2,1,0:T(8,128)} %get-tuple-element.45), channel_id=1, source_target_pairs={{16,32},{32,16},{48,64},{64,48},{80,96},{96,80},{112,128},{128,112... | collective-permute-start | bytes 2359304 | tf_op jit(solution)/shard_map/ppermute | solution.py:447
  71.7 20.6 %collective-permute-start.7 = (f32[2,6,128,128]{3,2,1,0:T(8,128)}, f32[2,6,128,128]{3,2,1,0:T(8,128)S(1)}, u32[]{:S(2)}, u32[]{:S(2)}) collective-permute-start(f32[2,6,128,128]{3,2,1,0:T(8,128)} %get-tuple-element.46), channel_id=1, source_target_pairs={{0,16},{16,0},{32,48},{48,32},{64,80},{80,64},{96,112},{112,96},{1... | collective-permute-start | bytes 2359304 | tf_op jit(solution)/shard_map/ppermute | solution.py:447
  82.6 19.8 %all-to-all-start.1 = ((f32[8,6,8,128]{3,2,1,0:T(8,128)}), f32[8,6,8,128]{3,2,1,0:T(8,128)S(1)}, u32[]{:S(2)}, u32[]{:S(2)}) async-start(f32[8,6,8,128]{3,2,1,0:T(8,128)} %plane_sum.1), calls=%async_computation.1 | async-start | bytes 393216 | tf_op jit(solution)/shard_map/all_to_all | solution.py:473
  104.6 25.6 %collective-permute-start.8 = (f32[2,512,128]{2,1,0:T(8,128)}, f32[2,512,128]{2,1,0:T(8,128)}, u32[]{:S(2)}, u32[]{:S(2)}) collective-permute-start(f32[2,512,128]{2,1,0:T(8,128)} %get-tuple-element.49), channel_id=1, source_target_pairs={{1,2},{2,1},{3,4},{4,3},{5,6},{6,5},{7,8},{8,7},{9,10},{10,9},{11,... | collective-permute-start | bytes 1572872 | tf_op jit(solution)/shard_map/ppermute | solution.py:447
  106.1 24.2 %collective-permute-start.9 = (f32[2,512,128]{2,1,0:T(8,128)}, f32[2,512,128]{2,1,0:T(8,128)}, u32[]{:S(2)}, u32[]{:S(2)}) collective-permute-start(f32[2,512,128]{2,1,0:T(8,128)} %get-tuple-element.50), channel_id=1, source_target_pairs={{0,1},{1,0},{2,3},{3,2},{4,5},{5,4},{6,7},{7,6},{8,9},{9,8},{10,11... | collective-permute-start | bytes 1572872 | tf_op jit(solution)/shard_map/ppermute | solution.py:447
  109.7 19.7 %all-to-all-start.2 = ((f32[32,4,8,128]{3,2,1,0:T(8,128)}), f32[32,4,8,128]{3,2,1,0:T(8,128)S(1)}, u32[]{:S(2)}, u32[]{:S(2)}) async-start(f32[32,4,8,128]{3,2,1,0:T(8,128)} %probe_rows.1), calls=%async_computation.2 | async-start | bytes 1048576 | tf_op jit(solution)/shard_map/all_to_all | solution.py:473
